TPU v7x, 128 devices: a whole 4x4x4 slice. The times are simulated.
128 devices in a mesh: tm: 32 (over z, y, x_lo), slab: 4 (over x_hi, core).
Axes of the slice: x: 4 (x_hi: 2, x_lo: 2; x = x_hi * 2 + x_lo), y: 4, z: 4, core: 2. Of those that a mesh axis runs over, the one named last changes fastest.
Arguments:
- kspace: bfloat16 [2, 64, 4, 96, 9984], P(None, 'tm', None, 'slab'), may hold values from -40 to 40, as said below
- sens: float32 [2, 4, 8, 104, 96], P(None, None, None, 'slab'), may hold values from -3 to 3
Outputs:
- projected: float32 [64, 2, 8, 104, 96], P('tm', None, None, 'slab')
Inputs may be any that keep to these rules, and one draw needn't show every extreme that they name: `kspace`: k-space values of order one with frames of different scale.
All inputs are finite; a program needn't handle non-finite values.
Results may differ from a plain program's by a relative error of at most 0.0036.
Values may be sent and summed in bfloat16 or wider, within the bound.
A program may use at most 128 MiB of HBM per device.

v0:
```python
import jax
import jax.numpy as jnp
from jax import lax
from jax.sharding import PartitionSpec as P

NX = 96
NY = 104
NZ = 96
RANK = 32
ITERS = 4
XW = 8


def inverse_table(length, count, offset):
    outputs = jnp.arange(count, dtype=jnp.int32) + offset
    inputs = jnp.arange(length, dtype=jnp.int32)
    phase = outputs[:, None] * inputs[None, :] % length
    angle = phase.astype(jnp.float32) * (2.0 * jnp.pi / length)
    norm_factor = 1.0 / jnp.sqrt(jnp.float32(length))
    return (jnp.cos(angle) * norm_factor, jnp.sin(angle) * norm_factor)


def contract(pattern, matrix_table, operand):
    return jnp.einsum(pattern, matrix_table, operand, precision=lax.Precision.HIGHEST)


def matmul(left, right):
    return jnp.dot(left, right, precision=lax.Precision.HIGHEST)


def orthonormal(rows, gram):
    factor = jnp.linalg.cholesky(matmul(matmul(rows, gram), rows.T))
    return lax.linalg.triangular_solve(factor, rows, left_side=True, lower=True)


def local(kspace, sens):
    frames_dev = kspace.shape[1]
    coil_count = kspace.shape[2]
    depth_dev = kspace.shape[3]
    spectrum = kspace.astype(jnp.float32).reshape(2, frames_dev, coil_count, depth_dev, NX, NY)
    across_cos, across_sin = inverse_table(NX, XW, (NX - XW) // 2)
    down_cos, down_sin = inverse_table(NY, NY, 0)
    depth_cos, depth_sin = inverse_table(NZ, NZ, 0)
    across_real = contract("jx,fczxy->fczjy", across_cos, spectrum[0]) - contract(
        "jx,fczxy->fczjy", across_sin, spectrum[1]
    )
    across_other = contract("jx,fczxy->fczjy", across_cos, spectrum[1]) + contract(
        "jx,fczxy->fczjy", across_sin, spectrum[0]
    )
    down_real = contract("my,fczjy->fczjm", down_cos, across_real) - contract(
        "my,fczjy->fczjm", down_sin, across_other
    )
    down_other = contract("my,fczjy->fczjm", down_cos, across_other) + contract(
        "my,fczjy->fczjm", down_sin, across_real
    )
    planes = jnp.stack([down_real, down_other]).astype(jnp.bfloat16)
    arrived = lax.all_to_all(planes, "slab", split_axis=5, concat_axis=3, tiled=True).astype(
        jnp.float32
    )
    depth_real = contract("wz,fczxy->fcxyw", depth_cos, arrived[0]) - contract(
        "wz,fczxy->fcxyw", depth_sin, arrived[1]
    )
    depth_other = contract("wz,fczxy->fcxyw", depth_cos, arrived[1]) + contract(
        "wz,fczxy->fcxyw", depth_sin, arrived[0]
    )
    sens_real = sens[0][None]
    sens_other = sens[1][None]
    combined_real = jnp.sum(sens_real * depth_real + sens_other * depth_other, axis=1)
    combined_other = jnp.sum(sens_real * depth_other - sens_other * depth_real, axis=1)
    matrix = jnp.stack([combined_real, combined_other], axis=1).reshape(frames_dev, -1)
    rows = lax.all_to_all(matrix, "tm", split_axis=1, concat_axis=0, tiled=True)
    gram = lax.psum(matmul(rows, rows.T), ("tm", "slab"))
    eye = jnp.eye(RANK, dtype=jnp.float32)
    current = jnp.concatenate([eye, eye], axis=1)
    for sweep_index in range(ITERS):
        current = matmul(orthonormal(current, gram), gram)
    coeff = orthonormal(current, gram)
    mixing = matmul(matmul(coeff, gram).T, coeff)
    projected = matmul(mixing, rows)
    projected = lax.all_to_all(projected, "tm", split_axis=0, concat_axis=1, tiled=True)
    return projected.reshape(frames_dev, 2, XW, -1, NZ)


def solution(mesh):
    in_specs = (P(None, "tm", None, "slab", None), P(None, None, None, "slab", None))
    out_specs = P("tm", None, None, "slab", None)
    return jax.shard_map(local, mesh=mesh, in_specs=in_specs, out_specs=out_specs, check_vma=False)
```

profile of v0, /device:TPU:0, one launch (start us, length us, event | category | flops | bytes accessed | tf_op | source)
XLA Modules:
  0.0 234.5 jit_solution(5598859404871233806)
XLA Ops:
  0.0 5.4 %fusion.180 = (bf16[1,2,4,24,9984]{4,3,2,1,0:T(8,128)(2,1)}, bf16[1,2,4,24,9984]{4,3,2,1,0:T(8,128)(2,1)}) fusion(bf16[2,2,4,24,9984]{4,3,2,1,0:T(8,128)(2,1)} %param.5), kind=kLoop, calls=%fused_computation.213 | loop fusion | bytes 15335424 | tf_op jit(solution)/shard_map/slice | solution.py:44
  5.4 13.7 %squeeze.16 = bf16[2,4,24,96,104]{4,3,2,1,0:T(8,128)(2,1)} reshape(bf16[1,2,4,24,9984]{4,3,2,1,0:T(8,128)(2,1)} %get-tuple-element.9) | data formatting | bytes 7667712 | tf_op jit(solution)/shard_map/squeeze | solution.py:44
  19.2 13.8 %squeeze.17 = bf16[2,4,24,96,104]{4,3,2,1,0:T(8,128)(2,1)} reshape(bf16[1,2,4,24,9984]{4,3,2,1,0:T(8,128)(2,1)} %get-tuple-element.10) | data formatting | bytes 7667712 | tf_op jit(solution)/shard_map/squeeze | solution.py:45
  33.0 4.3 %fusion.105 = f32[8,2,4,24,104]{4,0,3,2,1:T(8,128)S(1)} fusion(bf16[2,4,24,96,104]{4,3,2,1,0:T(8,128)(2,1)} %squeeze.16, s32[8]{0:T(128)S(1)} %iota_add_fusion), kind=kOutput, calls=%fused_computation.133 | convolution fusion | flops 184032768 | bytes 4472864 | tf_op jit(solution)/shard_map/jx,fczxy->fczjy/dot_general | solution.py:24
  37.3 2.1 fusion.103
  39.4 2.1 fusion.1
  42.5 2.1 fusion
  48.6 5.8 %copy.42 = bf16[2,2,4,24,8,104]{3,4,2,1,0,5:T(8,128)(2,1)S(1)} copy(bf16[2,2,4,24,8,104]{5,3,4,2,1,0:T(8,128)(2,1)} %pad_maximum_fusion) | data formatting | bytes 1277952 | tf_op jit(solution)/shard_map/stack | solution.py:56
  54.4 5.0 %reshape.64 = bf16[4,2,39936]{2,1,0:T(2,128)(2,1)} reshape(bf16[104,2,2,4,8,24]{5,4,3,2,1,0:T(8,128)(2,1)S(1)} %bitcast.164) | data formatting | bytes 1277952
  59.4 4.4 %all-to-all-start = ((bf16[4,2,39936]{2,1,0:T(2,128)(2,1)}), bf16[4,2,39936]{2,1,0:T(2,128)(2,1)}, u32[]{:S(2)}, u32[]{:S(2)}) async-start(bf16[4,2,39936]{2,1,0:T(2,128)(2,1)} %reshape.64), calls=%async_computation | async-start | bytes 1277952 | tf_op jit(solution)/shard_map/all_to_all | solution.py:57
  66.8 8.7 %all-to-all-done = bf16[4,2,39936]{2,1,0:T(2,128)(2,1)} async-done(((bf16[4,2,39936]{2,1,0:T(2,128)(2,1)}), bf16[4,2,39936]{2,1,0:T(2,128)(2,1)}, u32[]{:S(2)}, u32[]{:S(2)}) %all-to-all-start) | async-done | bytes 639008 | tf_op jit(solution)/shard_map/all_to_all | solution.py:57
  75.5 5.6 %reshape.65 = bf16[104,2,2,4,8,24]{5,4,3,2,1,0:T(8,128)(2,1)S(1)} reshape(bf16[4,2,39936]{2,1,0:T(2,128)(2,1)} %all-to-all-done) | data formatting | bytes 1277952
  81.1 4.4 %copy.86 = bf16[2,2,4,24,8,4,26]{3,5,4,6,2,1,0:T(4,128)(2,1)S(1)} copy(bf16[2,2,4,24,8,4,26]{3,4,2,1,0,6,5:T(8,128)(2,1)S(1)} %bitcast.165) | data formatting | bytes 1277952 | tf_op jit(solution)/shard_map/all_to_all | solution.py:57
  85.5 1.2 fusion.181
  86.7 1.6 squeeze.18
  88.3 2.9 %fusion.16 = f32[2,4,8,26,96]{4,3,2,1,0:T(8,128)} fusion(bf16[2,4,96,8,26]{2,3,4,1,0:T(8,128)(2,1)} %squeeze.18), kind=kOutput, calls=%fused_computation.27 | convolution fusion | flops 184117248 | bytes 958464 | tf_op jit(solution)/shard_map/wz,fczxy->fcxyw/dot_general | solution.py:24
  92.8 2.0 convolution_subtract_fusion
  94.9 2.2 add_reduce_fusion
  98.3 9.4 %all-to-all-start.1 = ((f32[2,32,1248]{2,0,1:T(2,128)}), f32[2,32,1248]{2,0,1:T(2,128)S(1)}, u32[]{:S(2)}, u32[]{:S(2)}) async-start(f32[2,32,1248]{2,0,1:T(2,128)} %copy.49), calls=%async_computation.1 | async-start | bytes 655360 | tf_op jit(solution)/shard_map/all_to_all | solution.py:71
  107.7 9.6 %all-to-all-done.1 = f32[2,32,1248]{2,0,1:T(2,128)S(1)} async-done(((f32[2,32,1248]{2,0,1:T(2,128)}), f32[2,32,1248]{2,0,1:T(2,128)S(1)}, u32[]{:S(2)}, u32[]{:S(2)}) %all-to-all-start.1) | async-done | bytes 319520 | tf_op jit(solution)/shard_map/all_to_all | solution.py:71
  118.2 62.4 %psum.7 = f32[64,64]{1,0:T(8,128)S(1)} all-reduce(f32[64,64]{1,0:T(8,128)S(1)} %fusion.182), channel_id=1, replica_groups=mesh['tm'=32,'slab'=4] {'tm','slab'}, use_global_device_ids=true, to_apply=%region_2.3 | all-reduce | flops 4096 | bytes 32768 | tf_op jit(solution)/shard_map/psum | solution.py:72
  181.1 2.9 %cholesky.89 = f32[32,32]{1,0:T(8,128)S(1)} custom-call(f32[32,32]{1,0:T(8,128)S(1)} %fusion.89), custom_call_target="Cholesky" | custom-call | tf_op jit(solution)/shard_map/jit(cholesky)/cholesky | solution.py:32
  185.4 2.4 %custom-call.9 = f32[1,32,32]{1,2,0:T(8,128)S(1)} custom-call(f32[1,32,32]{2,1,0:T(8,128)S(1)} %fusion.70), custom_call_target="InvertDiagBlocksLowerTriangular" | custom-call | tf_op jit(solution)/shard_map/triangular_solve/custom-call.0 | solution.py:33
  188.6 2.9 %cholesky.100 = f32[32,32]{1,0:T(8,128)S(1)} custom-call(f32[32,32]{1,0:T(8,128)S(1)} %fusion.86), custom_call_target="Cholesky" | custom-call | tf_op jit(solution)/shard_map/jit(cholesky)/cholesky | solution.py:32
  192.9 2.4 %custom-call.10 = f32[1,32,32]{1,2,0:T(8,128)S(1)} custom-call(f32[1,32,32]{2,1,0:T(8,128)S(1)} %fusion.71), custom_call_target="InvertDiagBlocksLowerTriangular" | custom-call | tf_op jit(solution)/shard_map/triangular_solve/custom-call.0 | solution.py:33
  196.1 2.9 %cholesky.111 = f32[32,32]{1,0:T(8,128)S(1)} custom-call(f32[32,32]{1,0:T(8,128)S(1)} %fusion.83), custom_call_target="Cholesky" | custom-call | tf_op jit(solution)/shard_map/jit(cholesky)/cholesky | solution.py:32
  200.4 2.4 %custom-call.11 = f32[1,32,32]{1,2,0:T(8,128)S(1)} custom-call(f32[1,32,32]{2,1,0:T(8,128)S(1)} %fusion.72), custom_call_target="InvertDiagBlocksLowerTriangular" | custom-call | tf_op jit(solution)/shard_map/triangular_solve/custom-call.0 | solution.py:33
  203.6 2.9 %cholesky.122 = f32[32,32]{1,0:T(8,128)S(1)} custom-call(f32[32,32]{1,0:T(8,128)S(1)} %fusion.80), custom_call_target="Cholesky" | custom-call | tf_op jit(solution)/shard_map/jit(cholesky)/cholesky | solution.py:32
  207.8 2.4 %custom-call.12 = f32[1,32,32]{1,2,0:T(8,128)S(1)} custom-call(f32[1,32,32]{2,1,0:T(8,128)S(1)} %fusion.73), custom_call_target="InvertDiagBlocksLowerTriangular" | custom-call | tf_op jit(solution)/shard_map/triangular_solve/custom-call.0 | solution.py:33
  211.1 2.9 %cholesky.133 = f32[32,32]{1,0:T(8,128)S(1)} custom-call(f32[32,32]{1,0:T(8,128)S(1)} %fusion.77), custom_call_target="Cholesky" | custom-call | tf_op jit(solution)/shard_map/jit(cholesky)/cholesky | solution.py:32
  215.3 2.4 %custom-call.13 = f32[1,32,32]{1,2,0:T(8,128)S(1)} custom-call(f32[1,32,32]{2,1,0:T(8,128)S(1)} %fusion.74), custom_call_target="InvertDiagBlocksLowerTriangular" | custom-call | tf_op jit(solution)/shard_map/triangular_solve/custom-call.0 | solution.py:33
  219.1 14.0 %all_to_all.47 = f32[32,2,1248]{2,1,0:T(2,128)S(1)} all-to-all(f32[32,2,1248]{2,1,0:T(2,128)S(1)} %copy.56), channel_id=1, replica_groups=mesh['tm'=32,'slab'=4] {'tm'}, dimensions={0} | all-to-all | bytes 638976 | tf_op jit(solution)/shard_map/all_to_all | solution.py:80
  (80 shorter events, 24.6 us)
Async XLA Ops:
  33.0 4.3 %copy-start = (bf16[2,4,24,96,104]{4,3,2,1,0:T(8,128)(2,1)S(1)}, bf16[2,4,24,96,104]{4,3,2,1,0:T(8,128)(2,1)}, u32[]{:S(2)}) copy-start(bf16[2,4,24,96,104]{4,3,2,1,0:T(8,128)(2,1)} %squeeze.17) | copy-start | bytes 11501572
  37.3 5.1 %slice-start = ((s8[4718592]{0:T(1024)(128)(4,1)}), s8[4194304]{0:T(1024)(128)(4,1)S(1)}, s32[]{:S(2)}) async-start(s8[4718592]{0:T(1024)(128)(4,1)} %bitcast.161), calls=%async_computation.3 | async-start | bytes 8388608
  39.4 3.1 %slice-start.1 = ((s8[4718592]{0:T(1024)(128)(4,1)}), s8[524288]{0:T(1024)(128)(4,1)S(1)}, s32[]{:S(2)}) async-start(s8[4718592]{0:T(1024)(128)(4,1)} %bitcast.161), calls=%async_computation.4 | async-start | bytes 1048576
  59.4 16.1 %all-to-all-start = ((bf16[4,2,39936]{2,1,0:T(2,128)(2,1)}), bf16[4,2,39936]{2,1,0:T(2,128)(2,1)}, u32[]{:S(2)}, u32[]{:S(2)}) async-start(bf16[4,2,39936]{2,1,0:T(2,128)(2,1)} %reshape.64), calls=%async_computation | async-start | bytes 1277952 | tf_op jit(solution)/shard_map/all_to_all | solution.py:57
  88.3 6.6 %copy-start.1 = (bf16[2,4,96,8,26]{2,3,4,1,0:T(8,128)(2,1)S(1)}, bf16[2,4,96,8,26]{2,3,4,1,0:T(8,128)(2,1)}, u32[]{:S(2)}) copy-start(bf16[2,4,96,8,26]{2,3,4,1,0:T(8,128)(2,1)} %squeeze.18) | copy-start | bytes 958468
  88.3 6.6 %copy-start.2 = (f32[4,8,26,96]{3,2,1,0:T(8,128)S(1)}, f32[4,8,26,96]{3,2,1,0:T(8,128)}, u32[]{:S(2)}) copy-start(f32[4,8,26,96]{3,2,1,0:T(8,128)} %copy.37) | copy-start | bytes 958468
  98.3 19.0 %all-to-all-start.1 = ((f32[2,32,1248]{2,0,1:T(2,128)}), f32[2,32,1248]{2,0,1:T(2,128)S(1)}, u32[]{:S(2)}, u32[]{:S(2)}) async-start(f32[2,32,1248]{2,0,1:T(2,128)} %copy.49), calls=%async_computation.1 | async-start | bytes 655360 | tf_op jit(solution)/shard_map/all_to_all | solution.py:71
where the time goes:
time: 235 us; the launch traced here: 234 us
  blocking collectives  76.4 us (33%)
  local copies, waits for them, and re-layouts  64.1 us (27%)
  other arithmetic  34.6 us (15%)
  matrix products  26.8 us (11%)
  waiting for transfers between devices  18.3 us (8%)
  starting transfers between devices  13.7 us (6%)
    psum x1, blocking collectives, local(): gram = lax.psum(matmul(rows, rows.T), ('tm', 'slab'))  62.4 us
    dot_general x12, matrix products, contract(): jnp.einsum(pattern, matrix_table, operand, precision=lax.Precision.HIGHEST)  22.3 us
    another operation x16, other arithmetic, orthonormal(): factor = jnp.linalg.cholesky(matmul(matmul(rows, gram), rows.T))  18 us
    another operation x10, other arithmetic, orthonormal(): return lax.linalg.triangular_solve(factor, rows, left_side=True, lower=True)  15.4 us
    all_to_all x1, blocking collectives, local(): lax.all_to_all(projected, 'tm', split_axis=0, concat_axis=1, tiled=True)  14 us
    squeeze x1, local copies, waits for them, and re-layouts, local(): spectrum[1]  13.8 us
    squeeze x1, local copies, waits for them, and re-layouts, local(): spectrum[0]  13.7 us
    unnamed x12, local copies, waits for them, and re-layouts  10.6 us
  transfers between devices with their start and end apart: 2, of which 2 were waited for; matrix products, arithmetic and copies ran while one was open for 1% of the time, Pallas kernels for 0%

commit v1 on v0

--- a/solution.py
+++ b/solution.py
@@ -69,7 +69,7 @@
     combined_other = jnp.sum(sens_real * depth_other - sens_other * depth_real, axis=1)
     matrix = jnp.stack([combined_real, combined_other], axis=1).reshape(frames_dev, -1)
     rows = lax.all_to_all(matrix, "tm", split_axis=1, concat_axis=0, tiled=True)
-    gram = lax.psum(matmul(rows, rows.T), ("tm", "slab"))
+    gram = jax.lax.psum(jax.lax.psum(matmul(rows, rows.T), "tm"), "slab")
     eye = jnp.eye(RANK, dtype=jnp.float32)
     current = jnp.concatenate([eye, eye], axis=1)
     for sweep_index in range(ITERS):

time: 235 us -> 340 us (1.45)
  blocking collectives: 76.4 us -> 181 us
    psum x1 -> x2, blocking collectives: 62.4 us -> 168 us  [local(): gram = jax.lax.psum(jax.lax.psum(matmul(rows, rows.T), 'tm'), 'slab')]
where the time goes in v1:
time: 340 us; the launch traced here: 339 us
  blocking collectives  181 us (53%)
  local copies, waits for them, and re-layouts  64.1 us (19%)
  other arithmetic  34.6 us (10%)
  matrix products  26.8 us (8%)
  waiting for transfers between devices  18.3 us (5%)
  starting transfers between devices  13.7 us (4%)
    psum x2, blocking collectives, local(): gram = jax.lax.psum(jax.lax.psum(matmul(rows, rows.T), 'tm'), 'slab')  168 us
    dot_general x12, matrix products, contract(): jnp.einsum(pattern, matrix_table, operand, precision=lax.Precision.HIGHEST)  22.3 us
    another operation x16, other arithmetic, orthonormal(): factor = jnp.linalg.cholesky(matmul(matmul(rows, gram), rows.T))  18 us
    another operation x10, other arithmetic, orthonormal(): return lax.linalg.triangular_solve(factor, rows, left_side=True, lower=True)  15.4 us
    squeeze x1, local copies, waits for them, and re-layouts, local(): spectrum[1]  13.8 us
    squeeze x1, local copies, waits for them, and re-layouts, local(): spectrum[0]  13.7 us
    all_to_all x1, blocking collectives, local(): lax.all_to_all(projected, 'tm', split_axis=0, concat_axis=1, tiled=True)  13.3 us
    unnamed x12, local copies, waits for them, and re-layouts  10.6 us
  transfers between devices with their start and end apart: 2, of which 2 were waited for; matrix products, arithmetic and copies ran while one was open for 1% of the time, Pallas kernels for 0%

profile of v1, /device:TPU:0, one launch (start us, length us, event | category | flops | bytes accessed | tf_op | source)
XLA Modules:
  0.0 339.2 jit_solution(6064368612708245236)
XLA Ops:
  0.0 5.4 %fusion.180 = (bf16[1,2,4,24,9984]{4,3,2,1,0:T(8,128)(2,1)}, bf16[1,2,4,24,9984]{4,3,2,1,0:T(8,128)(2,1)}) fusion(bf16[2,2,4,24,9984]{4,3,2,1,0:T(8,128)(2,1)} %param.5), kind=kLoop, calls=%fused_computation.213 | loop fusion | bytes 15335424 | tf_op jit(solution)/shard_map/slice | solution.py:44
  5.4 13.7 %squeeze.16 = bf16[2,4,24,96,104]{4,3,2,1,0:T(8,128)(2,1)} reshape(bf16[1,2,4,24,9984]{4,3,2,1,0:T(8,128)(2,1)} %get-tuple-element.9) | data formatting | bytes 7667712 | tf_op jit(solution)/shard_map/squeeze | solution.py:44
  19.2 13.8 %squeeze.17 = bf16[2,4,24,96,104]{4,3,2,1,0:T(8,128)(2,1)} reshape(bf16[1,2,4,24,9984]{4,3,2,1,0:T(8,128)(2,1)} %get-tuple-element.10) | data formatting | bytes 7667712 | tf_op jit(solution)/shard_map/squeeze | solution.py:45
  33.0 4.3 %fusion.105 = f32[8,2,4,24,104]{4,0,3,2,1:T(8,128)S(1)} fusion(bf16[2,4,24,96,104]{4,3,2,1,0:T(8,128)(2,1)} %squeeze.16, s32[8]{0:T(128)S(1)} %iota_add_fusion), kind=kOutput, calls=%fused_computation.133 | convolution fusion | flops 184032768 | bytes 4472864 | tf_op jit(solution)/shard_map/jx,fczxy->fczjy/dot_general | solution.py:24
  37.3 2.1 fusion.103
  39.4 2.1 fusion.1
  42.5 2.1 fusion
  48.6 5.8 %copy.42 = bf16[2,2,4,24,8,104]{3,4,2,1,0,5:T(8,128)(2,1)S(1)} copy(bf16[2,2,4,24,8,104]{5,3,4,2,1,0:T(8,128)(2,1)} %pad_maximum_fusion) | data formatting | bytes 1277952 | tf_op jit(solution)/shard_map/stack | solution.py:56
  54.4 5.0 %reshape.64 = bf16[4,2,39936]{2,1,0:T(2,128)(2,1)} reshape(bf16[104,2,2,4,8,24]{5,4,3,2,1,0:T(8,128)(2,1)S(1)} %bitcast.164) | data formatting | bytes 1277952
  59.4 4.4 %all-to-all-start = ((bf16[4,2,39936]{2,1,0:T(2,128)(2,1)}), bf16[4,2,39936]{2,1,0:T(2,128)(2,1)}, u32[]{:S(2)}, u32[]{:S(2)}) async-start(bf16[4,2,39936]{2,1,0:T(2,128)(2,1)} %reshape.64), calls=%async_computation | async-start | bytes 1277952 | tf_op jit(solution)/shard_map/all_to_all | solution.py:57
  66.8 8.7 %all-to-all-done = bf16[4,2,39936]{2,1,0:T(2,128)(2,1)} async-done(((bf16[4,2,39936]{2,1,0:T(2,128)(2,1)}), bf16[4,2,39936]{2,1,0:T(2,128)(2,1)}, u32[]{:S(2)}, u32[]{:S(2)}) %all-to-all-start) | async-done | bytes 639008 | tf_op jit(solution)/shard_map/all_to_all | solution.py:57
  75.5 5.6 %reshape.65 = bf16[104,2,2,4,8,24]{5,4,3,2,1,0:T(8,128)(2,1)S(1)} reshape(bf16[4,2,39936]{2,1,0:T(2,128)(2,1)} %all-to-all-done) | data formatting | bytes 1277952
  81.1 4.4 %copy.86 = bf16[2,2,4,24,8,4,26]{3,5,4,6,2,1,0:T(4,128)(2,1)S(1)} copy(bf16[2,2,4,24,8,4,26]{3,4,2,1,0,6,5:T(8,128)(2,1)S(1)} %bitcast.165) | data formatting | bytes 1277952 | tf_op jit(solution)/shard_map/all_to_all | solution.py:57
  86.7 1.6 squeeze.18
  88.3 2.9 fusion.16
  92.8 2.0 convolution_subtract_fusion
  94.9 2.2 add_reduce_fusion
  98.3 9.4 %all-to-all-start.1 = ((f32[2,32,1248]{2,0,1:T(2,128)}), f32[2,32,1248]{2,0,1:T(2,128)S(1)}, u32[]{:S(2)}, u32[]{:S(2)}) async-start(f32[2,32,1248]{2,0,1:T(2,128)} %copy.49), calls=%async_computation.1 | async-start | bytes 655360 | tf_op jit(solution)/shard_map/all_to_all | solution.py:71
  107.7 9.6 %all-to-all-done.1 = f32[2,32,1248]{2,0,1:T(2,128)S(1)} async-done(((f32[2,32,1248]{2,0,1:T(2,128)}), f32[2,32,1248]{2,0,1:T(2,128)S(1)}, u32[]{:S(2)}, u32[]{:S(2)}) %all-to-all-start.1) | async-done | bytes 319520 | tf_op jit(solution)/shard_map/all_to_all | solution.py:71
  118.2 154.7 %psum.14 = f32[64,64]{1,0:T(8,128)S(1)} all-reduce(f32[64,64]{1,0:T(8,128)S(1)} %fusion.182), channel_id=1, replica_groups=mesh['tm'=32,'slab'=4] {'tm'}, use_global_device_ids=true, to_apply=%region_2.3 | all-reduce | flops 4096 | bytes 32768 | tf_op jit(solution)/shard_map/psum | solution.py:72
  272.9 13.3 %psum.15 = f32[64,64]{1,0:T(8,128)S(1)} all-reduce(f32[64,64]{1,0:T(8,128)S(1)} %psum.14), channel_id=1, replica_groups=mesh['tm'=32,'slab'=4] {'slab'}, use_global_device_ids=true, to_apply=%region_3.4 | all-reduce | flops 4096 | bytes 32768 | tf_op jit(solution)/shard_map/psum | solution.py:72
  286.7 2.9 cholesky.89
  290.9 2.4 custom-call.9
  294.2 2.9 cholesky.100
  298.4 2.4 custom-call.10
  301.7 2.9 cholesky.111
  305.9 2.4 custom-call.11
  309.1 2.9 cholesky.122
  313.4 2.4 custom-call.12
  316.6 2.9 cholesky.133
  320.9 2.4 custom-call.13
  324.7 13.3 %all_to_all.47 = f32[32,2,1248]{2,1,0:T(2,128)S(1)} all-to-all(f32[32,2,1248]{2,1,0:T(2,128)S(1)} %copy.56), channel_id=1, replica_groups=mesh['tm'=32,'slab'=4] {'tm'}, dimensions={0} | all-to-all | bytes 638976 | tf_op jit(solution)/shard_map/all_to_all | solution.py:80
  (81 shorter events, 25.8 us)
Async XLA Ops:
  33.0 4.3 %copy-start = (bf16[2,4,24,96,104]{4,3,2,1,0:T(8,128)(2,1)S(1)}, bf16[2,4,24,96,104]{4,3,2,1,0:T(8,128)(2,1)}, u32[]{:S(2)}) copy-start(bf16[2,4,24,96,104]{4,3,2,1,0:T(8,128)(2,1)} %squeeze.17) | copy-start | bytes 11501572
  37.3 5.1 %slice-start = ((s8[4718592]{0:T(1024)(128)(4,1)}), s8[4194304]{0:T(1024)(128)(4,1)S(1)}, s32[]{:S(2)}) async-start(s8[4718592]{0:T(1024)(128)(4,1)} %bitcast.161), calls=%async_computation.3 | async-start | bytes 8388608
  39.4 3.1 slice-start.1
  59.4 16.1 %all-to-all-start = ((bf16[4,2,39936]{2,1,0:T(2,128)(2,1)}), bf16[4,2,39936]{2,1,0:T(2,128)(2,1)}, u32[]{:S(2)}, u32[]{:S(2)}) async-start(bf16[4,2,39936]{2,1,0:T(2,128)(2,1)} %reshape.64), calls=%async_computation | async-start | bytes 1277952 | tf_op jit(solution)/shard_map/all_to_all | solution.py:57
  88.3 6.6 %copy-start.1 = (bf16[2,4,96,8,26]{2,3,4,1,0:T(8,128)(2,1)S(1)}, bf16[2,4,96,8,26]{2,3,4,1,0:T(8,128)(2,1)}, u32[]{:S(2)}) copy-start(bf16[2,4,96,8,26]{2,3,4,1,0:T(8,128)(2,1)} %squeeze.18) | copy-start | bytes 958468
  88.3 6.6 %copy-start.2 = (f32[4,8,26,96]{3,2,1,0:T(8,128)S(1)}, f32[4,8,26,96]{3,2,1,0:T(8,128)}, u32[]{:S(2)}) copy-start(f32[4,8,26,96]{3,2,1,0:T(8,128)} %copy.37) | copy-start | bytes 958468
  98.3 19.0 %all-to-all-start.1 = ((f32[2,32,1248]{2,0,1:T(2,128)}), f32[2,32,1248]{2,0,1:T(2,128)S(1)}, u32[]{:S(2)}, u32[]{:S(2)}) async-start(f32[2,32,1248]{2,0,1:T(2,128)} %copy.49), calls=%async_computation.1 | async-start | bytes 655360 | tf_op jit(solution)/shard_map/all_to_all | solution.py:71
